TPU v7x, 32 devices: a whole 2x2x4 slice. The times are simulated.
32 devices in a mesh: groups: 2 (over x), row: 8 (over z, y), col: 2 (over core).
Axes of the slice: x: 2, y: 2, z: 4, core: 2. Of those that a mesh axis runs over, the one named last changes fastest.
Arguments:
- density: float32 [192, 10, 128, 128], P(('groups', 'row', 'col')), parts along dimension 0, may hold values from -0.5 to 0.5
- pattern_table: int32 [64, 96, 10], replicated, may hold values from 0 to 95, as said below
- structure_id: int32 [2], P('groups'), parts along dimension 0, may hold values from 0 to 63
Outputs:
- purified: float32 [192, 10, 128, 128], P(('groups', 'row', 'col')), parts along dimension 0
There are 2 independent parts, one for each index of `groups`. A program takes and returns all parts, laid end to end along the dimension named above; an argument that names none is the same for every part. Nothing has to cross between parts.
Inputs may be any that keep to these rules, and one draw needn't show every extreme that they name: pattern_table[s, i, 0] = i; the 10 entries of a row are distinct, and each differs from i, modulo 96, by at most 12.
All inputs are finite; a program needn't handle non-finite values.
Results may differ from a plain program's by a relative error of at most 0.0003.
Values sent between devices are 32-bit elements; how exact they have to be, the bound alone decides.
A program may use at most 128 MiB of HBM per device.

v0:
```python
import jax
import jax.numpy as jnp
from jax import lax
from jax.sharding import PartitionSpec as P

HOPS = 2


def passed_along(shard, axis, by):
    size = lax.axis_size(axis)
    return lax.ppermute(shard, axis, [(i, (i + by) % size) for i in range(size)])


def purify_row(flat_window, window_first, pattern, own_blocks, global_row):
    total_rows = pattern.shape[0]
    blocks = pattern.shape[1]
    width = own_blocks.shape[1]
    columns = lax.dynamic_index_in_dim(pattern, global_row, 0, keepdims=False)
    where_rows = jnp.mod(columns - window_first, total_rows)
    fetched_cols = pattern[columns]
    matches = fetched_cols[:, :, None] == columns[None, None, :]
    slot_ids = jnp.arange(blocks, dtype=jnp.int32)
    chosen = jnp.sum(jnp.where(matches, slot_ids[None, :, None], 0), axis=1)
    present = jnp.any(matches, axis=1)
    flat_index = where_rows[:, None] * blocks + chosen
    picked = flat_window[flat_index.T]
    linked = jnp.where(present.T[:, :, None, None], picked, jnp.zeros_like(picked))
    linked = linked.reshape(blocks, blocks * width, width)
    own_wide = jnp.transpose(own_blocks, (1, 0, 2)).reshape(width, blocks * width)
    square = jnp.einsum("xk,cky->cxy", own_wide, linked, precision=lax.Precision.HIGHEST)
    square_wide = jnp.transpose(square, (1, 0, 2)).reshape(width, blocks * width)
    cube = jnp.einsum("xk,cky->cxy", square_wide, linked, precision=lax.Precision.HIGHEST)
    return 3.0 * square - 2.0 * cube


def body(density, pattern_table, structure_id):
    rows_dev = density.shape[0]
    pattern = lax.dynamic_index_in_dim(pattern_table, structure_id[0], 0, keepdims=False)
    total_rows = pattern.shape[0]
    pieces = []
    for offset in range(HOPS, -HOPS - 1, -1):
        pieces.append(density if offset == 0 else passed_along(density, ("row", "col"), offset))
    window_first = (lax.axis_index(("row", "col")) - HOPS) * rows_dev
    window = jnp.concatenate(pieces, axis=0)
    flat_window = window.reshape(-1, window.shape[2], window.shape[3])
    window_first = jnp.mod(window_first, total_rows)
    first_row = lax.axis_index(("row", "col")) * rows_dev

    def one_row(inputs):
        own_blocks, local_row = inputs
        return purify_row(flat_window, window_first, pattern, own_blocks, first_row + local_row)

    return lax.map(one_row, (density, jnp.arange(rows_dev, dtype=jnp.int32)))


def solution(mesh):
    return jax.shard_map(
        body,
        mesh=mesh,
        in_specs=(P(("groups", "row", "col"), None, None, None), P(), P("groups")),
        out_specs=P(("groups", "row", "col"), None, None, None),
        check_vma=False,
    )
```

profile of v0, /device:TPU:0, one launch (start us, length us, event | category | flops | bytes accessed | tf_op | source)
XLA Modules:
  0.0 479.9 jit_solution(18120159977401153418)
XLA Ops:
  0.0 3.0 collective-permute-start
  3.0 4.4 collective-permute-start.2
  8.6 206.4 %collective-permute-done = f32[6,10,128,128]{3,2,1,0:T(8,128)} collective-permute-done((f32[6,10,128,128]{3,2,1,0:T(8,128)}, f32[6,10,128,128]{3,2,1,0:T(8,128)}, u32[]{:S(2)}, u32[]{:S(2)}) %collective-permute-start) | collective-permute-done | bytes 3932192 | tf_op jit(solution)/shard_map/ppermute | solution.py:11
  217.6 2.6 constant_dynamic-update-slice_fusion.4
  220.7 2.6 constant_dynamic-update-slice_fusion.2
  223.3 36.5 %collective-permute-done.3 = f32[6,10,128,128]{3,2,1,0:T(8,128)} collective-permute-done((f32[6,10,128,128]{3,2,1,0:T(8,128)}, f32[6,10,128,128]{3,2,1,0:T(8,128)}, u32[]{:S(2)}, u32[]{:S(2)}) %collective-permute-start.3) | collective-permute-done | bytes 3932192 | tf_op jit(solution)/shard_map/ppermute | solution.py:11
  262.4 6.7 %copy-done.2 = f32[30,10,128,128]{3,2,1,0:T(8,128)} copy-done((f32[30,10,128,128]{3,2,1,0:T(8,128)}, f32[30,10,128,128]{3,2,1,0:T(8,128)S(1)}, u32[]{:S(2)}) %copy-start.2) | copy-done | bytes 19660824
  269.1 210.8 %while.12 = (s32[]{:T(128)}, f32[6,10,128,128]{3,2,1,0:T(8,128)}, s32[6]{0:T(128)S(1)}, s32[]{:T(128)}, s32[96,10]{1,0:T(8,128)S(1)}, /*index=5*/s32[]{:T(128)},...) while((s32[]{:T(128)}, f32[6,10,128,128]{3,2,1,0:T(8,128)}, ...), condition=%wide.region_3.4_spmd, body=%wide.region_0.3_spmd.sunk | while | flops 5036940288 | bytes 70794400 | solution.py:53
  271.2 10.3 %gather_fusion.1 = f32[100,128,128]{2,1,0:T(8,128)} fusion(f32[300,128,128]{2,1,0:T(8,128)} %get-tuple-element.207, s32[1024]{0:T(1024)S(1)} %pad_clamp_fusion.5), kind=kCustom, calls=%fused_computation.1.clone.1 | custom fusion | bytes 13107600 | tf_op jit(solution)/shard_map/while/body/eval_jaxpr/gather | solution.py:26
  281.5 8.1 %copy.25 = f32[10,10,128,128]{2,3,1,0:T(8,128)} copy(f32[10,10,128,128]{3,2,1,0:T(8,128)} %bitcast.71) | data formatting | bytes 13107200 | tf_op jit(solution)/shard_map/while/body/eval_jaxpr/gather | solution.py:26
  289.9 7.8 %fusion.47 = f32[10,128,128,1]{2,1,3,0:T(8,128)S(1)} fusion(f32[10,10,128,128]{2,3,1,0:T(8,128)} %copy.25, pred[10,10]{1,0:T(8,128)(4,1)S(1)} %copy.26, f32[6,10,128,128]{3,2,1,0:T(8,128)} %get-tuple-element.208, s32[]{:T(128)} %get-tuple-element.190), kind=kOutput, calls=%fused_computation.4.clone.1 | convolution fusion | flops 2518220800 | bytes 7864932 | tf_op jit(solution)/shard_map/while/body/eval_jaxpr/xk,cky->cxy/dot_general | solution.py:30
  297.7 5.4 %fusion.48 = f32[1,10,128,128]{2,3,1,0:T(8,128)S(1)} fusion(f32[10,10,128,128]{2,3,1,0:T(8,128)S(1)} %copy-done.1, pred[10,10]{1,0:T(8,128)(4,1)S(1)} %copy.26, f32[10,128,128,1]{2,1,3,0:T(8,128)S(1)} %fusion.47), kind=kOutput, calls=%fused_computation.13.clone.1 | convolution fusion | flops 2518712320 | bytes 7864420 | tf_op jit(solution)/shard_map/while/body/eval_jaxpr/xk,cky->cxy/dot_general | solution.py:32
  306.4 10.3 %gather_fusion.1 = f32[100,128,128]{2,1,0:T(8,128)} fusion(f32[300,128,128]{2,1,0:T(8,128)} %get-tuple-element.207, s32[1024]{0:T(1024)S(1)} %pad_clamp_fusion.5), kind=kCustom, calls=%fused_computation.1.clone.1 | custom fusion | bytes 13107600 | tf_op jit(solution)/shard_map/while/body/eval_jaxpr/gather | solution.py:26
  316.7 8.1 %copy.25 = f32[10,10,128,128]{2,3,1,0:T(8,128)} copy(f32[10,10,128,128]{3,2,1,0:T(8,128)} %bitcast.71) | data formatting | bytes 13107200 | tf_op jit(solution)/shard_map/while/body/eval_jaxpr/gather | solution.py:26
  325.0 7.8 %fusion.47 = f32[10,128,128,1]{2,1,3,0:T(8,128)S(1)} fusion(f32[10,10,128,128]{2,3,1,0:T(8,128)} %copy.25, pred[10,10]{1,0:T(8,128)(4,1)S(1)} %copy.26, f32[6,10,128,128]{3,2,1,0:T(8,128)} %get-tuple-element.208, s32[]{:T(128)} %get-tuple-element.190), kind=kOutput, calls=%fused_computation.4.clone.1 | convolution fusion | flops 2518220800 | bytes 7864932 | tf_op jit(solution)/shard_map/while/body/eval_jaxpr/xk,cky->cxy/dot_general | solution.py:30
  332.8 5.4 %fusion.48 = f32[1,10,128,128]{2,3,1,0:T(8,128)S(1)} fusion(f32[10,10,128,128]{2,3,1,0:T(8,128)S(1)} %copy-done.1, pred[10,10]{1,0:T(8,128)(4,1)S(1)} %copy.26, f32[10,128,128,1]{2,1,3,0:T(8,128)S(1)} %fusion.47), kind=kOutput, calls=%fused_computation.13.clone.1 | convolution fusion | flops 2518712320 | bytes 7864420 | tf_op jit(solution)/shard_map/while/body/eval_jaxpr/xk,cky->cxy/dot_general | solution.py:32
  341.5 10.3 %gather_fusion.1 = f32[100,128,128]{2,1,0:T(8,128)} fusion(f32[300,128,128]{2,1,0:T(8,128)} %get-tuple-element.207, s32[1024]{0:T(1024)S(1)} %pad_clamp_fusion.5), kind=kCustom, calls=%fused_computation.1.clone.1 | custom fusion | bytes 13107600 | tf_op jit(solution)/shard_map/while/body/eval_jaxpr/gather | solution.py:26
  351.8 8.1 %copy.25 = f32[10,10,128,128]{2,3,1,0:T(8,128)} copy(f32[10,10,128,128]{3,2,1,0:T(8,128)} %bitcast.71) | data formatting | bytes 13107200 | tf_op jit(solution)/shard_map/while/body/eval_jaxpr/gather | solution.py:26
  360.2 7.8 %fusion.47 = f32[10,128,128,1]{2,1,3,0:T(8,128)S(1)} fusion(f32[10,10,128,128]{2,3,1,0:T(8,128)} %copy.25, pred[10,10]{1,0:T(8,128)(4,1)S(1)} %copy.26, f32[6,10,128,128]{3,2,1,0:T(8,128)} %get-tuple-element.208, s32[]{:T(128)} %get-tuple-element.190), kind=kOutput, calls=%fused_computation.4.clone.1 | convolution fusion | flops 2518220800 | bytes 7864932 | tf_op jit(solution)/shard_map/while/body/eval_jaxpr/xk,cky->cxy/dot_general | solution.py:30
  368.0 5.4 %fusion.48 = f32[1,10,128,128]{2,3,1,0:T(8,128)S(1)} fusion(f32[10,10,128,128]{2,3,1,0:T(8,128)S(1)} %copy-done.1, pred[10,10]{1,0:T(8,128)(4,1)S(1)} %copy.26, f32[10,128,128,1]{2,1,3,0:T(8,128)S(1)} %fusion.47), kind=kOutput, calls=%fused_computation.13.clone.1 | convolution fusion | flops 2518712320 | bytes 7864420 | tf_op jit(solution)/shard_map/while/body/eval_jaxpr/xk,cky->cxy/dot_general | solution.py:32
  376.6 10.3 %gather_fusion.1 = f32[100,128,128]{2,1,0:T(8,128)} fusion(f32[300,128,128]{2,1,0:T(8,128)} %get-tuple-element.207, s32[1024]{0:T(1024)S(1)} %pad_clamp_fusion.5), kind=kCustom, calls=%fused_computation.1.clone.1 | custom fusion | bytes 13107600 | tf_op jit(solution)/shard_map/while/body/eval_jaxpr/gather | solution.py:26
  386.9 8.1 %copy.25 = f32[10,10,128,128]{2,3,1,0:T(8,128)} copy(f32[10,10,128,128]{3,2,1,0:T(8,128)} %bitcast.71) | data formatting | bytes 13107200 | tf_op jit(solution)/shard_map/while/body/eval_jaxpr/gather | solution.py:26
  395.3 7.8 %fusion.47 = f32[10,128,128,1]{2,1,3,0:T(8,128)S(1)} fusion(f32[10,10,128,128]{2,3,1,0:T(8,128)} %copy.25, pred[10,10]{1,0:T(8,128)(4,1)S(1)} %copy.26, f32[6,10,128,128]{3,2,1,0:T(8,128)} %get-tuple-element.208, s32[]{:T(128)} %get-tuple-element.190), kind=kOutput, calls=%fused_computation.4.clone.1 | convolution fusion | flops 2518220800 | bytes 7864932 | tf_op jit(solution)/shard_map/while/body/eval_jaxpr/xk,cky->cxy/dot_general | solution.py:30
  403.1 5.4 %fusion.48 = f32[1,10,128,128]{2,3,1,0:T(8,128)S(1)} fusion(f32[10,10,128,128]{2,3,1,0:T(8,128)S(1)} %copy-done.1, pred[10,10]{1,0:T(8,128)(4,1)S(1)} %copy.26, f32[10,128,128,1]{2,1,3,0:T(8,128)S(1)} %fusion.47), kind=kOutput, calls=%fused_computation.13.clone.1 | convolution fusion | flops 2518712320 | bytes 7864420 | tf_op jit(solution)/shard_map/while/body/eval_jaxpr/xk,cky->cxy/dot_general | solution.py:32
  411.8 10.3 %gather_fusion.1 = f32[100,128,128]{2,1,0:T(8,128)} fusion(f32[300,128,128]{2,1,0:T(8,128)} %get-tuple-element.207, s32[1024]{0:T(1024)S(1)} %pad_clamp_fusion.5), kind=kCustom, calls=%fused_computation.1.clone.1 | custom fusion | bytes 13107600 | tf_op jit(solution)/shard_map/while/body/eval_jaxpr/gather | solution.py:26
  422.1 8.1 %copy.25 = f32[10,10,128,128]{2,3,1,0:T(8,128)} copy(f32[10,10,128,128]{3,2,1,0:T(8,128)} %bitcast.71) | data formatting | bytes 13107200 | tf_op jit(solution)/shard_map/while/body/eval_jaxpr/gather | solution.py:26
  430.4 7.8 %fusion.47 = f32[10,128,128,1]{2,1,3,0:T(8,128)S(1)} fusion(f32[10,10,128,128]{2,3,1,0:T(8,128)} %copy.25, pred[10,10]{1,0:T(8,128)(4,1)S(1)} %copy.26, f32[6,10,128,128]{3,2,1,0:T(8,128)} %get-tuple-element.208, s32[]{:T(128)} %get-tuple-element.190), kind=kOutput, calls=%fused_computation.4.clone.1 | convolution fusion | flops 2518220800 | bytes 7864932 | tf_op jit(solution)/shard_map/while/body/eval_jaxpr/xk,cky->cxy/dot_general | solution.py:30
  438.2 5.4 %fusion.48 = f32[1,10,128,128]{2,3,1,0:T(8,128)S(1)} fusion(f32[10,10,128,128]{2,3,1,0:T(8,128)S(1)} %copy-done.1, pred[10,10]{1,0:T(8,128)(4,1)S(1)} %copy.26, f32[10,128,128,1]{2,1,3,0:T(8,128)S(1)} %fusion.47), kind=kOutput, calls=%fused_computation.13.clone.1 | convolution fusion | flops 2518712320 | bytes 7864420 | tf_op jit(solution)/shard_map/while/body/eval_jaxpr/xk,cky->cxy/dot_general | solution.py:32
  446.9 10.3 %gather_fusion.1 = f32[100,128,128]{2,1,0:T(8,128)} fusion(f32[300,128,128]{2,1,0:T(8,128)} %get-tuple-element.207, s32[1024]{0:T(1024)S(1)} %pad_clamp_fusion.5), kind=kCustom, calls=%fused_computation.1.clone.1 | custom fusion | bytes 13107600 | tf_op jit(solution)/shard_map/while/body/eval_jaxpr/gather | solution.py:26
  457.2 8.1 %copy.25 = f32[10,10,128,128]{2,3,1,0:T(8,128)} copy(f32[10,10,128,128]{3,2,1,0:T(8,128)} %bitcast.71) | data formatting | bytes 13107200 | tf_op jit(solution)/shard_map/while/body/eval_jaxpr/gather | solution.py:26
  465.6 7.8 %fusion.47 = f32[10,128,128,1]{2,1,3,0:T(8,128)S(1)} fusion(f32[10,10,128,128]{2,3,1,0:T(8,128)} %copy.25, pred[10,10]{1,0:T(8,128)(4,1)S(1)} %copy.26, f32[6,10,128,128]{3,2,1,0:T(8,128)} %get-tuple-element.208, s32[]{:T(128)} %get-tuple-element.190), kind=kOutput, calls=%fused_computation.4.clone.1 | convolution fusion | flops 2518220800 | bytes 7864932 | tf_op jit(solution)/shard_map/while/body/eval_jaxpr/xk,cky->cxy/dot_general | solution.py:30
  473.4 5.4 %fusion.48 = f32[1,10,128,128]{2,3,1,0:T(8,128)S(1)} fusion(f32[10,10,128,128]{2,3,1,0:T(8,128)S(1)} %copy-done.1, pred[10,10]{1,0:T(8,128)(4,1)S(1)} %copy.26, f32[10,128,128,1]{2,1,3,0:T(8,128)S(1)} %fusion.47), kind=kOutput, calls=%fused_computation.13.clone.1 | convolution fusion | flops 2518712320 | bytes 7864420 | tf_op jit(solution)/shard_map/while/body/eval_jaxpr/xk,cky->cxy/dot_general | solution.py:32
  (112 shorter events, 23.3 us)
Async XLA Ops:
  0.0 8.5 %copy-start = (s32[64,96,10]{1,0,2:T(8,128)S(1)}, s32[64,96,10]{1,0,2:T(8,128)}, u32[]{:S(2)}) copy-start(s32[64,96,10]{1,0,2:T(8,128)} %param.6) | copy-start | bytes 737284
  0.0 215.0 %collective-permute-start = (f32[6,10,128,128]{3,2,1,0:T(8,128)}, f32[6,10,128,128]{3,2,1,0:T(8,128)}, u32[]{:S(2)}, u32[]{:S(2)}) collective-permute-start(f32[6,10,128,128]{3,2,1,0:T(8,128)} %param.5), channel_id=1, source_target_pairs={{0,2},{1,3},{2,4},{3,5},{4,6},{5,7},{6,8},{7,9},{8,10},{9,11},{10,... | collective-permute-start | bytes 11796488 | tf_op jit(solution)/shard_map/ppermute | solution.py:11
  3.0 214.6 %collective-permute-start.1 = (f32[6,10,128,128]{3,2,1,0:T(8,128)}, f32[6,10,128,128]{3,2,1,0:T(8,128)}, u32[]{:S(2)}, u32[]{:S(2)}) collective-permute-start(f32[6,10,128,128]{3,2,1,0:T(8,128)} %param.5), channel_id=1, source_target_pairs={{0,1},{1,2},{2,3},{3,4},{4,5},{5,6},{6,7},{7,8},{8,9},{9,10},{10,1... | collective-permute-start | bytes 11796488 | tf_op jit(solution)/shard_map/ppermute | solution.py:11
  3.0 217.7 %collective-permute-start.2 = (f32[6,10,128,128]{3,2,1,0:T(8,128)}, f32[6,10,128,128]{3,2,1,0:T(8,128)}, u32[]{:S(2)}, u32[]{:S(2)}) collective-permute-start(f32[6,10,128,128]{3,2,1,0:T(8,128)} %param.5), channel_id=1, source_target_pairs={{0,15},{1,0},{2,1},{3,2},{4,3},{5,4},{6,5},{7,6},{8,7},{9,8},{10,9... | collective-permute-start | bytes 11796488 | tf_op jit(solution)/shard_map/ppermute | solution.py:11
  7.4 252.4 %collective-permute-start.3 = (f32[6,10,128,128]{3,2,1,0:T(8,128)}, f32[6,10,128,128]{3,2,1,0:T(8,128)}, u32[]{:S(2)}, u32[]{:S(2)}) collective-permute-start(f32[6,10,128,128]{3,2,1,0:T(8,128)} %param.5), channel_id=1, source_target_pairs={{0,14},{1,15},{2,0},{3,1},{4,2},{5,3},{6,4},{7,5},{8,6},{9,7},{10,... | collective-permute-start | bytes 11796488 | tf_op jit(solution)/shard_map/ppermute | solution.py:11
  8.6 211.6 %copy-start.3 = (f32[6,10,128,128]{3,2,1,0:T(8,128)S(1)}, f32[6,10,128,128]{3,2,1,0:T(8,128)}, u32[]{:S(2)}) copy-start(f32[6,10,128,128]{3,2,1,0:T(8,128)} %param.5) | copy-start | bytes 11796484
  262.4 6.7 %copy-start.2 = (f32[30,10,128,128]{3,2,1,0:T(8,128)}, f32[30,10,128,128]{3,2,1,0:T(8,128)S(1)}, u32[]{:S(2)}) copy-start(f32[30,10,128,128]{3,2,1,0:T(8,128)S(1)} %constant_dynamic-update-slice_fusion.1) | copy-start | bytes 58982404
  289.9 7.8 %copy-start.1 = (f32[10,10,128,128]{2,3,1,0:T(8,128)S(1)}, f32[10,10,128,128]{2,3,1,0:T(8,128)}, u32[]{:S(2)}) copy-start(f32[10,10,128,128]{2,3,1,0:T(8,128)} %copy.25) | copy-start | bytes 19660804 | tf_op jit(solution)/shard_map/while
  325.0 7.8 %copy-start.1 = (f32[10,10,128,128]{2,3,1,0:T(8,128)S(1)}, f32[10,10,128,128]{2,3,1,0:T(8,128)}, u32[]{:S(2)}) copy-start(f32[10,10,128,128]{2,3,1,0:T(8,128)} %copy.25) | copy-start | bytes 19660804 | tf_op jit(solution)/shard_map/while
  360.2 7.8 %copy-start.1 = (f32[10,10,128,128]{2,3,1,0:T(8,128)S(1)}, f32[10,10,128,128]{2,3,1,0:T(8,128)}, u32[]{:S(2)}) copy-start(f32[10,10,128,128]{2,3,1,0:T(8,128)} %copy.25) | copy-start | bytes 19660804 | tf_op jit(solution)/shard_map/while
  395.3 7.8 %copy-start.1 = (f32[10,10,128,128]{2,3,1,0:T(8,128)S(1)}, f32[10,10,128,128]{2,3,1,0:T(8,128)}, u32[]{:S(2)}) copy-start(f32[10,10,128,128]{2,3,1,0:T(8,128)} %copy.25) | copy-start | bytes 19660804 | tf_op jit(solution)/shard_map/while
  430.4 7.8 %copy-start.1 = (f32[10,10,128,128]{2,3,1,0:T(8,128)S(1)}, f32[10,10,128,128]{2,3,1,0:T(8,128)}, u32[]{:S(2)}) copy-start(f32[10,10,128,128]{2,3,1,0:T(8,128)} %copy.25) | copy-start | bytes 19660804 | tf_op jit(solution)/shard_map/while
  465.6 7.8 %copy-start.1 = (f32[10,10,128,128]{2,3,1,0:T(8,128)S(1)}, f32[10,10,128,128]{2,3,1,0:T(8,128)}, u32[]{:S(2)}) copy-start(f32[10,10,128,128]{2,3,1,0:T(8,128)} %copy.25) | copy-start | bytes 19660804 | tf_op jit(solution)/shard_map/while
where the time goes:
time: 483 us; the launch traced here: 480 us
  waiting for transfers between devices  243 us (50%)
  local copies, waits for them, and re-layouts  144 us (30%)
  matrix products  79 us (16%)
  starting transfers between devices  7.81 us (2%)
    ppermute x4, waiting for transfers between devices, passed_along(): lax.ppermute(shard, axis, [(i, (i + by) % size) for i in range(size)])  243 us
    gather x12, local copies, waits for them, and re-layouts, purify_row(): picked = flat_window[flat_index.T]  111 us
    dot_general x6, matrix products, purify_row(): jnp.einsum('xk,cky->cxy', own_wide, linked, precision=lax.Precision.HIGHEST)  46.6 us
    dot_general x6, matrix products, purify_row(): jnp.einsum('xk,cky->cxy', square_wide, linked, precision=lax.Precision.HI...  32.4 us
    unnamed x10, local copies, waits for them, and re-layouts  14.9 us
  transfers between devices with their start and end apart: 4, of which 2 were waited for; matrix products, arithmetic and copies ran while one was open for 2% of the time, Pallas kernels for 0%

commit v1 on v0

v1 whole, which is shorter than its diff:
```python
import functools

import jax
import jax.numpy as jnp
from jax import lax
from jax.experimental import pallas as pl
from jax.experimental.pallas import tpu as pltpu
from jax.sharding import PartitionSpec as P

PIECE = 5
AHEAD = 3
LAG = 2
MESH = pl.DeviceIdType.MESH


def spread_kernel(chips, pieces, own, partner, across, onward, far,
                  p_send, p_recv, y_send, y_recv, z_send, z_recv, x_send, x_recv):
    chip = lax.axis_index("row")
    core = lax.axis_index("col")
    even = lax.rem(chip, 2) == 0
    step = jnp.where(even, 1, -1)
    paired = {"row": chip + step}
    target = {"row": lax.rem(chip + 2 * step + chips, chips)}
    source = {"row": lax.rem(chip - 2 * step + chips, chips)}
    other = {"col": 1 - core}

    barrier = pltpu.get_barrier_semaphore()
    for device in (paired, target, source, other):
        pl.semaphore_signal(barrier, inc=1, device_id=device, device_id_type=MESH)
    pl.semaphore_wait(barrier, 4)

    def copy(src, dst, send, recv, device):
        return pltpu.make_async_remote_copy(
            src_ref=src, dst_ref=dst, send_sem=send, recv_sem=recv,
            device_id=device, device_id_type=MESH)

    def part(n):
        return pl.ds(n * PIECE, PIECE)

    whole = copy(own, partner, p_send, p_recv, other)
    ys = [copy(own.at[part(n)], across.at[part(n)], y_send.at[n], y_recv.at[n], paired)
          for n in range(pieces)]
    zs = [copy(across.at[part(n)], onward.at[part(n)], z_send.at[n], z_recv.at[n], target)
          for n in range(pieces)]
    xy = [copy(across.at[part(n)], far.at[part(n)], x_send.at[n], x_recv.at[n], other)
          for n in range(pieces)]
    xz = [copy(onward.at[part(n)], far.at[part(n)], x_send.at[n], x_recv.at[n], other)
          for n in range(pieces)]
    from_across = lax.rem(chip, 2) == core

    def onward_arrived(n):
        zs[n].wait_recv()

        @pl.when(jnp.logical_not(from_across))
        def _():
            xz[n].start()

    for n in range(min(AHEAD, pieces)):
        ys[n].start()
    whole.start()
    for n in range(pieces):
        ys[n].wait_recv()
        zs[n].start()

        @pl.when(from_across)
        def _():
            xy[n].start()

        if n + AHEAD < pieces:
            ys[n].wait_send()
            ys[n + AHEAD].start()
        if n >= LAG:
            onward_arrived(n - LAG)
    for n in range(max(pieces - LAG, 0), pieces):
        onward_arrived(n)
    for n in range(pieces):
        if n + AHEAD >= pieces:
            ys[n].wait_send()
        zs[n].wait_send()
        xy[n].wait()
    whole.wait()


def spread(blocks, chips):
    pieces = blocks.shape[0] // PIECE
    dma = pltpu.SemaphoreType.DMA
    shard = jax.ShapeDtypeStruct(blocks.shape, blocks.dtype)
    return pl.pallas_call(
        functools.partial(spread_kernel, chips, pieces),
        out_shape=[shard] * 4,
        in_specs=[pl.BlockSpec(memory_space=pl.ANY)],
        out_specs=[pl.BlockSpec(memory_space=pl.ANY)] * 4,
        scratch_shapes=[dma, dma] + [dma((pieces,))] * 6,
        compiler_params=pltpu.CompilerParams(collective_id=0, has_side_effects=True),
    )(blocks)


def purify_kernel(rows, slots, where, own, partner, across, onward, far, out,
                  stage, high, low, wide, square, square_wide, sem):
    shards = (own, partner, across, onward, far)
    held = rows * slots
    half = held // 2
    width = out.shape[-1]
    jobs = [(s, h) for s in range(len(shards)) for h in range(2)]

    def load(n):
        s, h = jobs[n]
        return pltpu.make_async_copy(
            shards[s].at[pl.ds(h * half, half)], stage.at[n % 2], sem.at[n % 2])

    def halves(x):
        top = x.astype(jnp.bfloat16)
        return top, (x - top.astype(jnp.float32)).astype(jnp.bfloat16)

    load(0).start()
    high[len(shards) * held] = jnp.zeros((width, width), jnp.bfloat16)
    low[len(shards) * held] = jnp.zeros((width, width), jnp.bfloat16)
    for n in range(len(jobs)):
        if n + 1 < len(jobs):
            load(n + 1).start()
        load(n).wait()

        def split_one(b, _):
            top, rest = halves(stage[n % 2, b])
            high[n * half + b] = top
            low[n * half + b] = rest
            return 0

        lax.fori_loop(0, half, split_one, 0, unroll=2)

    def product(factor, row, c):
        tops, rests = [], []
        for a in range(slots):
            places = [where[(row * slots + a) * slots + c + k] for k in range(2)]
            tops.append(jnp.concatenate([high[p] for p in places], axis=1))
            rests.append(jnp.concatenate([low[p] for p in places], axis=1))
        both = jnp.dot(factor[...], jnp.concatenate(tops, axis=0),
                       preferred_element_type=jnp.float32)
        small = jnp.dot(factor[:width], jnp.concatenate(rests, axis=0),
                        preferred_element_type=jnp.float32)
        return both[:width] + (both[width:] + small)

    def one_row(row, _):
        for a in range(slots):
            columns = slice(a * width, (a + 1) * width)
            wide[:width, columns] = high[row * slots + a]
            wide[width:, columns] = low[row * slots + a]
        for c in range(0, slots, 2):
            columns = slice(c * width, (c + 2) * width)
            result = product(wide, row, c)
            square[:, columns] = result
            top, rest = halves(result)
            square_wide[:width, columns] = top
            square_wide[width:, columns] = rest
        for c in range(0, slots, 2):
            columns = slice(c * width, (c + 2) * width)
            result = 3.0 * square[:, columns] - 2.0 * product(square_wide, row, c)
            out[row, c] = result[:, :width]
            out[row, c + 1] = result[:, width:]
        return 0

    lax.fori_loop(0, rows, one_row, 0)


def purify(where, shards, rows, slots):
    held, width, _ = shards[0].shape
    count = len(shards) * held + 1
    vmem, narrow = pltpu.VMEM, jnp.bfloat16
    return pl.pallas_call(
        functools.partial(purify_kernel, rows, slots),
        out_shape=jax.ShapeDtypeStruct((rows, slots, width, width), jnp.float32),
        in_specs=[pl.BlockSpec(memory_space=pltpu.SMEM)]
        + [pl.BlockSpec(memory_space=pl.ANY)] * len(shards),
        out_specs=pl.BlockSpec(memory_space=vmem),
        scratch_shapes=[
            vmem((2, held // 2, width, width), jnp.float32),
            vmem((count, width, width), narrow),
            vmem((count, width, width), narrow),
            vmem((2 * width, slots * width), narrow),
            vmem((width, slots * width), jnp.float32),
            vmem((2 * width, slots * width), narrow),
            pltpu.SemaphoreType.DMA((2,)),
        ],
        compiler_params=pltpu.CompilerParams(vmem_limit_bytes=50 * 1024 * 1024),
    )(where, *shards)


def block_places(pattern, rows, chip, core):
    total, slots = pattern.shape
    first = (2 * chip + core) * rows
    own = lax.dynamic_slice_in_dim(pattern, first, rows, 0)
    fetched = pattern[own]
    matches = fetched[:, :, None, :] == own[:, None, :, None]
    slot = jnp.sum(jnp.where(matches, jnp.arange(slots, dtype=jnp.int32), 0), axis=3)
    present = jnp.any(matches, axis=3)
    frame = jnp.mod(own - (2 * chip - 2) * rows, total)
    group, local = frame // rows, frame % rows
    from_across = jnp.where(chip % 2 == 0, group >= 4, group < 2)
    shard = jnp.where(group == 2 + core, 0,
            jnp.where(group == 3 - core, 1,
            jnp.where(group == 1 + 3 * core, 4,
            jnp.where(from_across, 2, 3))))
    base = (shard * rows + local) * slots
    return jnp.where(present, base[:, :, None] + slot, 5 * rows * slots).reshape(-1)


def body(density, pattern_table, structure_id):
    rows, slots, width, _ = density.shape
    chip, core = lax.axis_index("row"), lax.axis_index("col")
    pattern = lax.dynamic_index_in_dim(pattern_table, structure_id[0], 0, keepdims=False)
    where = block_places(pattern, rows, chip, core)
    blocks = density.reshape(rows * slots, width, width)
    shards = (blocks, *spread(blocks, lax.axis_size("row")))
    return purify(where, shards, rows, slots)


def solution(mesh):
    return jax.shard_map(
        body,
        mesh=mesh,
        in_specs=(P(("groups", "row", "col"), None, None, None), P(), P("groups")),
        out_specs=P(("groups", "row", "col"), None, None, None),
        check_vma=False,
    )
```

time: 483 us -> 140 us (0.29)
  waiting for transfers between devices: 243 us -> 0 us
  local copies, waits for them, and re-layouts: 144 us -> 3.79 us
  Pallas kernels: 0 us -> 131 us
  matrix products: 79 us -> 0 us
  starting transfers between devices: 7.81 us -> 0 us
    ppermute x4 -> x0, waiting for transfers between devices: 243 us -> none  [passed_along(): lax.ppermute(shard, axis, [(i, (i + by) % size) for i in range(size)])]
    pallas_call x0 -> x2, Pallas kernels: none -> 131 us  [the longest x1 101 us: spread(): pl.pallas_call(functools.partial(spread_kernel, chips, pieces), out_shape...]
    gather x18 -> x3, local copies, waits for them, and re-layouts: 114 us -> 0.61 us  [block_places(): fetched = pattern[own]]
    dot_general x12 -> x0, matrix products: 79 us -> none  [the longest x6 46.6 us: purify_row(): jnp.einsum('xk,cky->cxy', own_wide, linked, precision=lax.Precision.HIGHEST)]
    unnamed x10 -> x5, local copies, waits for them, and re-layouts: 14.9 us -> 2.48 us
    ppermute x4 -> x0, starting transfers between devices: 7.81 us -> none  [passed_along(): lax.ppermute(shard, axis, [(i, (i + by) % size) for i in range(size)])]
    dynamic_update_slice x12 -> x0, local copies, waits for them, and re-layouts: 6.73 us -> none  [body(): return lax.map(one_row, (density, jnp.arange(rows_dev, dtype=jnp.int32)))]
  transfers between devices with their start and end apart: 4 -> 0, of which waited for: 2 -> 0; matrix products, arithmetic and copies ran while one was open for 2% -> 0% of each run, Pallas kernels for 0% -> 0%
where the time goes in v1:
time: 140 us
  Pallas kernels  131 us (94%)
  local copies, waits for them, and re-layouts  3.79 us (3%)
  other arithmetic  3.78 us (3%)
    pallas_call x1, Pallas kernels, spread(): pl.pallas_call(functools.partial(spread_kernel, chips, pieces), out_shape...  101 us
    pallas_call x1, Pallas kernels, purify(): pl.pallas_call(functools.partial(purify_kernel, rows, slots), out_shape=j...  30 us

profile of v1, /device:TPU:0, one launch (start us, length us, event | category | flops | bytes accessed | tf_op | source)
XLA Modules:
  0.0 139.6 jit_solution(8080222695580081422)
XLA Ops:
  0.0 0.0 copy-start
  0.7 0.3 copy-done
  1.0 0.1 constant_dynamic-slice_fusion
  1.1 0.1 copy.19
  1.2 0.1 reshape.81
  1.3 0.1 copy.15
  1.4 0.1 copy.10
  1.5 0.6 gather_fusion
  2.2 1.9 %compare_reduce_fusion = pred[6,10,10]{0,2,1:T(8,128)(4,1)S(1)} fusion(s32[6,10]{0,1:T(8,128)S(1)} %bitcast.18, s32[6,10,10]{2,0,1:T(8,128)S(1)} %copy.13), kind=kLoop, calls=%fused_computation.2 | loop fusion | flops 11400 | bytes 3240 | tf_op jit(solution)/shard_map/reduce_or | solution.py:195
  4.0 1.8 %fusion = s32[6,10,10]{0,2,1:T(8,128)S(1)} fusion(s32[6,10]{0,1:T(8,128)S(1)} %bitcast.19, s32[6,10,10]{2,0,1:T(8,128)S(1)} %copy.13), kind=kLoop, calls=%fused_computation.3 | loop fusion | flops 17400 | bytes 5040 | tf_op jit(solution)/shard_map/reduce_sum | solution.py:194
  5.9 0.2 copy.16
  6.1 0.1 select_n.126.where
  6.2 101.3 %shard_map.37 = (f32[60,128,128]{2,1,0:T(8,128)}, f32[60,128,128]{2,1,0:T(8,128)}, f32[60,128,128]{2,1,0:T(8,128)}, f32[60,128,128]{2,1,0:T(8,128)}) custom-call(f32[60,128,128]{2,1,0:T(8,128)} %bitcast.15), custom_call_target="tpu_custom_call" | custom-call | tf_op jit(solution)/shard_map/pallas_call | solution.py:88
  107.5 0.0 copy-start.1
  107.5 2.1 %copy-done.1 = f32[6,10,128,128]{3,2,1,0:T(8,128)S(1)} copy-done((f32[6,10,128,128]{3,2,1,0:T(8,128)S(1)}, f32[6,10,128,128]{3,2,1,0:T(8,128)}, u32[]{:S(2)}) %copy-start.1) | copy-done | bytes 3932184
  109.6 30.0 %shard_map.38 = f32[6,10,128,128]{3,2,1,0:T(8,128)} custom-call(s32[600]{0:T(1024)S(1)} %select_n.126.where, f32[60,128,128]{2,1,0:T(8,128)S(1)} %bitcast.16, f32[60,128,128]{2,1,0:T(8,128)} %get-tuple-element.9.partner, f32[60,128,128]{2,1,0:T(8,128)} %get-tuple-element.10.across, f32[60,128,128]{2,1,0:T(8,128)} %get-tuple-element.11.onward, ...), custom_call_target="tpu_custom_call" | custom-call | tf_op jit(solution)/shard_map/pallas_call | solution.py:169
  (8 shorter events, 0.1 us)
Async XLA Ops:
  0.0 1.0 copy-start
  107.5 2.1 %copy-start.1 = (f32[6,10,128,128]{3,2,1,0:T(8,128)S(1)}, f32[6,10,128,128]{3,2,1,0:T(8,128)}, u32[]{:S(2)}) copy-start(f32[6,10,128,128]{3,2,1,0:T(8,128)} %param.3) | copy-start | bytes 11796484

commit v2 on v0

v2 whole, which is shorter than its diff:
```python
import functools

import jax
import jax.numpy as jnp
from jax import lax
from jax.experimental import pallas as pl
from jax.experimental.pallas import tpu as pltpu
from jax.sharding import PartitionSpec as P

PIECE = 5
AHEAD = 3
LAG = 2
MESH = pl.DeviceIdType.MESH
OWN, PARTNER, ACROSS, ONWARD, FAR = range(5)
SHARDS = 5


def halves(x):
    top = x.astype(jnp.bfloat16)
    return top, (x - top.astype(jnp.float32)).astype(jnp.bfloat16)


def purify_kernel(chips, total, rows, slots, pattern, own, out,
                  partner, across, onward, far, high, low, square, wide, wider,
                  linked, factor, line,
                  p_send, p_recv, y_send, y_recv, z_send, z_recv, x_send, x_recv):
    width = out.shape[-1]
    held = rows * slots
    pieces = held // PIECE
    per_row = slots // PIECE
    lines = SHARDS * rows
    nothing = SHARDS * held
    chip = lax.axis_index("row")
    core = lax.axis_index("col")
    even = lax.rem(chip, 2) == 0
    step = jnp.where(even, 1, -1)
    paired = {"row": chip + step}
    target = {"row": lax.rem(chip + 2 * step + chips, chips)}
    source = {"row": lax.rem(chip - 2 * step + chips, chips)}
    other = {"col": 1 - core}

    barrier = pltpu.get_barrier_semaphore()
    for device in (paired, target, source, other):
        pl.semaphore_signal(barrier, inc=1, device_id=device, device_id_type=MESH)
    pl.semaphore_wait(barrier, 4)

    def copy(src, dst, send, recv, device):
        return pltpu.make_async_remote_copy(
            src_ref=src, dst_ref=dst, send_sem=send, recv_sem=recv,
            device_id=device, device_id_type=MESH)

    def part(n):
        return pl.ds(n * PIECE, PIECE)

    whole = copy(own, partner, p_send, p_recv, other)
    ys = [copy(own.at[part(n)], across.at[part(n)], y_send.at[n], y_recv.at[n], paired)
          for n in range(pieces)]
    zs = [copy(across.at[part(n)], onward.at[part(n)], z_send.at[n], z_recv.at[n], target)
          for n in range(pieces)]
    xy = [copy(across.at[part(n)], far.at[part(n)], x_send.at[n], x_recv.at[n], other)
          for n in range(pieces)]
    xz = [copy(onward.at[part(n)], far.at[part(n)], x_send.at[n], x_recv.at[n], other)
          for n in range(pieces)]
    from_across = lax.rem(chip, 2) == core

    for n in range(min(AHEAD, pieces)):
        ys[n].start()
    whole.start()

    def split(ref, shard, first, count):
        def one(b, _):
            top, rest = halves(ref[first + b])
            high[shard * held + first + b] = top
            low[shard * held + first + b] = rest
            return 0

        lax.fori_loop(0, count, one, 0)

    def wrapped(x):
        x = jnp.where(x < 0, x + total, x)
        return jnp.where(x >= total, x - total, x)

    mine = (2 * chip + core) * rows
    toward = chip + step
    away = lax.rem(chip - step + chips, chips)
    side = lax.rem(chip - 1 + 2 * core + chips, chips)
    firsts = [mine, (2 * chip + 1 - core) * rows, (2 * toward + core) * rows,
              (2 * away + core) * rows, (2 * side + 1 - core) * rows]

    def tabulate(row, _):
        columns = [pattern[(mine + row) * slots + a] for a in range(slots)]
        places = []
        for a in range(slots):
            place = jnp.int32(0)
            for shard, first in enumerate(firsts):
                off = wrapped(columns[a] - first)
                place = jnp.where(off < rows, shard * rows + off, place)
            line[row * slots + a] = place
            places.append(place)

        def one_line(m, _):
            shard, local = m // rows, m % rows
            at = jnp.int32(0)
            for s, first in enumerate(firsts):
                at = jnp.where(shard == s, first, at)
            at = wrapped(at + local)
            entries = [pattern[at * slots + b] for b in range(slots)]
            slot = jnp.int32(nothing)
            for a in range(slots):
                slot = jnp.where(places[a] == m, row * slots + a, slot)
            factor[row * lines + m] = slot
            for c in range(slots):
                found = jnp.int32(nothing)
                for b in range(slots):
                    found = jnp.where(entries[b] == columns[c], m * slots + b, found)
                linked[(row * lines + m) * slots + c] = found
            return 0

        lax.fori_loop(0, lines, one_line, 0)
        return 0

    def product(left, row, which, c):
        tops, rests = [], []
        for m in which:
            places = [linked[(row * lines + m) * slots + c + k] for k in range(2)]
            tops.append(jnp.concatenate([high[p] for p in places], axis=1))
            rests.append(jnp.concatenate([low[p] for p in places], axis=1))
        both = jnp.dot(left[:, :len(which) * width], jnp.concatenate(tops, axis=0),
                       preferred_element_type=jnp.float32)
        small = jnp.dot(left[:width, :len(which) * width], jnp.concatenate(rests, axis=0),
                        preferred_element_type=jnp.float32)
        return both[:width] + (both[width:] + small)

    def add_lines(which, begin, end, fresh=False):
        def one_row(row, _):
            for t, m in enumerate(which):
                place = factor[row * lines + m]
                wide[:width, t * width:(t + 1) * width] = high[place]
                wide[width:, t * width:(t + 1) * width] = low[place]
            for c in range(0, slots, 2):
                columns = slice(c * width, (c + 2) * width)
                result = product(wide, row, which, c)
                if fresh:
                    square[row, :, columns] = result
                else:
                    square[row, :, columns] += result
            return 0

        lax.fori_loop(begin, end, one_row, 0)

    def remote_lines(r):
        return [shard * rows + r for shard in (ACROSS, ONWARD, FAR)]

    def onward_arrived(n):
        zs[n].wait_recv()

        @pl.when(jnp.logical_not(from_across))
        def _():
            xz[n].start()

        split(onward, ONWARD, n * PIECE, PIECE)

    def far_arrived(n):
        xy[n].wait_recv()
        split(far, FAR, n * PIECE, PIECE)

    middle = rows // 2
    near = list(range(2 * rows))
    jobs = {}

    def at(n, job, *args):
        jobs.setdefault(n, []).append((job, args))

    def partner_arrived():
        whole.wait_recv()
        split(partner, PARTNER, 0, held)

    def tables(begin, end):
        lax.fori_loop(begin, end, tabulate, 0)

    at(0, tables, 0, rows // 3)
    at(1, tables, rows // 3, 2 * rows // 3)
    at(2, tables, 2 * rows // 3, rows)
    at(2, partner_arrived)
    at(3, add_lines, near, 0, middle, True)
    at(4, add_lines, near, middle, rows, True)
    for r in range(rows - 1):
        ready = (r + 1) * per_row + LAG + 1
        at(ready, add_lines, remote_lines(r), 0, middle)
        at(ready + 1, add_lines, remote_lines(r), middle, rows)

    high[nothing] = jnp.zeros((width, width), jnp.bfloat16)
    low[nothing] = jnp.zeros((width, width), jnp.bfloat16)
    split(own, OWN, 0, held)
    for n in range(pieces + LAG + 1):
        if n < pieces:
            ys[n].wait_recv()
            zs[n].start()

            @pl.when(from_across)
            def _():
                xy[n].start()

            if n + AHEAD < pieces:
                ys[n].wait_send()
                ys[n + AHEAD].start()
            split(across, ACROSS, n * PIECE, PIECE)
        if LAG <= n < pieces + LAG:
            onward_arrived(n - LAG)
        if n >= LAG + 1:
            far_arrived(n - LAG - 1)
        for job, args in jobs.pop(n, []):
            job(*args)
    for n in sorted(jobs):
        for job, args in jobs[n]:
            job(*args)
    add_lines(remote_lines(rows - 1), 0, rows)

    def finish(row, _):
        for c in range(0, slots, 2):
            columns = slice(c * width, (c + 2) * width)
            top, rest = halves(square[row, :, columns])
            wider[:width, columns] = top
            wider[width:, columns] = rest
        which = [line[row * slots + a] for a in range(slots)]
        for c in range(0, slots, 2):
            columns = slice(c * width, (c + 2) * width)
            result = 3.0 * square[row, :, columns] - 2.0 * product(wider, row, which, c)
            out[row, c] = result[:, :width]
            out[row, c + 1] = result[:, width:]
        return 0

    lax.fori_loop(0, rows, finish, 0)
    for n in range(pieces):
        if n + AHEAD >= pieces:
            ys[n].wait_send()
        zs[n].wait_send()
        xy[n].wait_send()
    whole.wait_send()


def body(density, pattern_table, structure_id):
    rows, slots, width, _ = density.shape
    total = pattern_table.shape[1]
    held = rows * slots
    pieces = held // PIECE
    pattern = lax.dynamic_index_in_dim(pattern_table, structure_id[0], 0, keepdims=False)
    blocks = density.reshape(held, width, width)
    dma, vmem, smem, narrow = pltpu.SemaphoreType.DMA, pltpu.VMEM, pltpu.SMEM, jnp.bfloat16
    lines = SHARDS * rows
    return pl.pallas_call(
        functools.partial(purify_kernel, lax.axis_size("row"), total, rows, slots),
        out_shape=jax.ShapeDtypeStruct(density.shape, density.dtype),
        in_specs=[pl.BlockSpec(memory_space=smem), pl.BlockSpec(memory_space=vmem)],
        out_specs=pl.BlockSpec(memory_space=vmem),
        scratch_shapes=[vmem(blocks.shape, blocks.dtype)] * 4
        + [vmem((SHARDS * held + 1, width, width), narrow)] * 2
        + [
            vmem((rows, width, slots * width), jnp.float32),
            vmem((2 * width, 2 * rows * width), narrow),
            vmem((2 * width, slots * width), narrow),
            smem((rows * lines * slots,), jnp.int32),
            smem((rows * lines,), jnp.int32),
            smem((rows * slots,), jnp.int32),
            dma, dma,
        ] + [dma((pieces,))] * 6,
        compiler_params=pltpu.CompilerParams(
            collective_id=0, has_side_effects=True, vmem_limit_bytes=56 * 1024 * 1024),
    )(pattern.reshape(-1), blocks)


def solution(mesh):
    return jax.shard_map(
        body,
        mesh=mesh,
        in_specs=(P(("groups", "row", "col"), None, None, None), P(), P("groups")),
        out_specs=P(("groups", "row", "col"), None, None, None),
        check_vma=False,
    )
```

time: 483 us -> 131 us (0.27)
  waiting for transfers between devices: 243 us -> 0 us
  local copies, waits for them, and re-layouts: 144 us -> 5.62 us
  Pallas kernels: 0 us -> 125 us
  matrix products: 79 us -> 0 us
  starting transfers between devices: 7.81 us -> 0 us
    ppermute x4 -> x0, waiting for transfers between devices: 243 us -> none  [passed_along(): lax.ppermute(shard, axis, [(i, (i + by) % size) for i in range(size)])]
    pallas_call x0 -> x1, Pallas kernels: none -> 125 us  [body(): pl.pallas_call(functools.partial(purify_kernel, lax.axis_size('row'), tot...]
    gather x18 -> x0, local copies, waits for them, and re-layouts: 114 us -> none  [the longest x12 111 us: purify_row(): picked = flat_window[flat_index.T]]
    dot_general x12 -> x0, matrix products: 79 us -> none  [the longest x6 46.6 us: purify_row(): jnp.einsum('xk,cky->cxy', own_wide, linked, precision=lax.Precision.HIGHEST)]
    unnamed x10 -> x3, local copies, waits for them, and re-layouts: 14.9 us -> 4.78 us
    ppermute x4 -> x0, starting transfers between devices: 7.81 us -> none  [passed_along(): lax.ppermute(shard, axis, [(i, (i + by) % size) for i in range(size)])]
    dynamic_update_slice x12 -> x0, local copies, waits for them, and re-layouts: 6.73 us -> none  [body(): return lax.map(one_row, (density, jnp.arange(rows_dev, dtype=jnp.int32)))]
  transfers between devices with their start and end apart: 4 -> 0, of which waited for: 2 -> 0; matrix products, arithmetic and copies ran while one was open for 2% -> 0% of each run, Pallas kernels for 0% -> 0%
where the time goes in v2:
time: 131 us
  Pallas kernels  125 us (95%)
  local copies, waits for them, and re-layouts  5.62 us (4%)
    pallas_call x1, Pallas kernels, body(): pl.pallas_call(functools.partial(purify_kernel, lax.axis_size('row'), tot...  125 us
    unnamed x3, local copies, waits for them, and re-layouts  4.78 us

profile of v2, /device:TPU:0, one launch (start us, length us, event | category | flops | bytes accessed | tf_op | source)
XLA Modules:
  0.0 131.2 jit_solution(4992474906783586666)
XLA Ops:
  0.0 0.0 copy-start
  0.7 0.3 copy-done
  1.0 0.1 copy.4
  1.1 0.7 reshape.7.pattern
  1.8 124.9 %shard_map.37 = f32[6,10,128,128]{3,2,1,0:T(8,128)} custom-call(s32[960]{0:T(1024)} %reshape.7.pattern, f32[60,128,128]{2,1,0:T(8,128)} %bitcast.5), custom_call_target="tpu_custom_call" | custom-call | tf_op jit(solution)/shard_map/pallas_call | solution.py:251
  126.8 4.5 %copy.7 = f32[6,10,128,128]{3,2,1,0:T(8,128)} copy(f32[6,10,128,128]{3,2,1,0:T(8,128)} %shard_map.37) | data formatting | bytes 7864320
  (1 shorter events, 0.0 us)
Async XLA Ops:
  0.0 1.0 copy-start

commit v3 on v2

--- a/solution.py
+++ b/solution.py
@@ -7,9 +7,9 @@
 from jax.experimental.pallas import tpu as pltpu
 from jax.sharding import PartitionSpec as P
 
-PIECE = 5
-AHEAD = 3
-LAG = 2
+PIECE = 2
+AHEAD = 8
+LAG = 3
 MESH = pl.DeviceIdType.MESH
 OWN, PARTNER, ACROSS, ONWARD, FAR = range(5)
 SHARDS = 5
@@ -21,9 +21,9 @@
 
 
 def purify_kernel(chips, total, rows, slots, pattern, own, out,
-                  partner, across, onward, far, high, low, square, wide, wider,
+                  held_own, partner, across, onward, far, done, high, low, square, wide, wider,
                   linked, factor, line,
-                  p_send, p_recv, y_send, y_recv, z_send, z_recv, x_send, x_recv):
+                  load_sem, out_sem, p_send, p_recv, y_send, y_recv, z_send, z_recv, x_send, x_recv):
     width = out.shape[-1]
     held = rows * slots
     pieces = held // PIECE
@@ -39,6 +39,8 @@
     source = {"row": lax.rem(chip - 2 * step + chips, chips)}
     other = {"col": 1 - core}
 
+    load = pltpu.make_async_copy(own, held_own, load_sem)
+    load.start()
     barrier = pltpu.get_barrier_semaphore()
     for device in (paired, target, source, other):
         pl.semaphore_signal(barrier, inc=1, device_id=device, device_id_type=MESH)
@@ -149,7 +151,8 @@
         lax.fori_loop(begin, end, one_row, 0)
 
     def remote_lines(r):
-        return [shard * rows + r for shard in (ACROSS, ONWARD, FAR)]
+        first = [ACROSS] if r == 0 else []
+        return [shard * rows + r for shard in first + [ONWARD, FAR]]
 
     def onward_arrived(n):
         zs[n].wait_recv()
@@ -164,12 +167,14 @@
         xy[n].wait_recv()
         split(far, FAR, n * PIECE, PIECE)
 
-    middle = rows // 2
-    near = list(range(2 * rows))
     jobs = {}
-
-    def at(n, job, *args):
-        jobs.setdefault(n, []).append((job, args))
+    free = 0
+
+    def then(ready, job, *args):
+        nonlocal free
+        free = max(ready, free)
+        jobs.setdefault(free, []).append((job, args))
+        free += 1
 
     def partner_arrived():
         whole.wait_recv()
@@ -178,20 +183,21 @@
     def tables(begin, end):
         lax.fori_loop(begin, end, tabulate, 0)
 
-    at(0, tables, 0, rows // 3)
-    at(1, tables, rows // 3, 2 * rows // 3)
-    at(2, tables, 2 * rows // 3, rows)
-    at(2, partner_arrived)
-    at(3, add_lines, near, 0, middle, True)
-    at(4, add_lines, near, middle, rows, True)
+    for begin in range(0, rows, 2):
+        then(0, tables, begin, min(begin + 2, rows))
+    then(0, partner_arrived)
+    middle = rows // 2
+    for begin, end in ((0, middle), (middle, rows)):
+        then(0, add_lines, list(range(2 * rows)), begin, end, True)
     for r in range(rows - 1):
-        ready = (r + 1) * per_row + LAG + 1
-        at(ready, add_lines, remote_lines(r), 0, middle)
-        at(ready + 1, add_lines, remote_lines(r), middle, rows)
+        group = remote_lines(r) + [ACROSS * rows + r + 1]
+        for begin, end in ((0, middle), (middle, rows)):
+            then((r + 2) * per_row - 1, add_lines, group, begin, end)
 
     high[nothing] = jnp.zeros((width, width), jnp.bfloat16)
     low[nothing] = jnp.zeros((width, width), jnp.bfloat16)
-    split(own, OWN, 0, held)
+    load.wait()
+    split(held_own, OWN, 0, held)
     for n in range(pieces + LAG + 1):
         if n < pieces:
             ys[n].wait_recv()
@@ -216,6 +222,9 @@
             job(*args)
     add_lines(remote_lines(rows - 1), 0, rows)
 
+    def leave(row):
+        return pltpu.make_async_copy(done.at[row], out.at[row], out_sem.at[row])
+
     def finish(row, _):
         for c in range(0, slots, 2):
             columns = slice(c * width, (c + 2) * width)
@@ -225,9 +234,10 @@
         which = [line[row * slots + a] for a in range(slots)]
         for c in range(0, slots, 2):
             columns = slice(c * width, (c + 2) * width)
-            result = 3.0 * square[row, :, columns] - 2.0 * product(wider, row, which, c)
-            out[row, c] = result[:, :width]
-            out[row, c + 1] = result[:, width:]
+            result = 1.5 * square[row, :, columns] - product(wider, row, which, c)
+            done[row, c] = result[:, :width]
+            done[row, c + 1] = result[:, width:]
+        leave(row).start()
         return 0
 
     lax.fori_loop(0, rows, finish, 0)
@@ -237,6 +247,8 @@
         zs[n].wait_send()
         xy[n].wait_send()
     whole.wait_send()
+    for row in range(rows):
+        leave(row).wait()
 
 
 def body(density, pattern_table, structure_id):
@@ -248,12 +260,13 @@
     blocks = density.reshape(held, width, width)
     dma, vmem, smem, narrow = pltpu.SemaphoreType.DMA, pltpu.VMEM, pltpu.SMEM, jnp.bfloat16
     lines = SHARDS * rows
-    return pl.pallas_call(
+    halved = pl.pallas_call(
         functools.partial(purify_kernel, lax.axis_size("row"), total, rows, slots),
         out_shape=jax.ShapeDtypeStruct(density.shape, density.dtype),
-        in_specs=[pl.BlockSpec(memory_space=smem), pl.BlockSpec(memory_space=vmem)],
-        out_specs=pl.BlockSpec(memory_space=vmem),
-        scratch_shapes=[vmem(blocks.shape, blocks.dtype)] * 4
+        in_specs=[pl.BlockSpec(memory_space=smem), pl.BlockSpec(memory_space=pl.ANY)],
+        out_specs=pl.BlockSpec(memory_space=pl.ANY),
+        scratch_shapes=[vmem(blocks.shape, blocks.dtype)] * 5
+        + [vmem(density.shape, density.dtype)]
         + [vmem((SHARDS * held + 1, width, width), narrow)] * 2
         + [
             vmem((rows, width, slots * width), jnp.float32),
@@ -262,11 +275,12 @@
             smem((rows * lines * slots,), jnp.int32),
             smem((rows * lines,), jnp.int32),
             smem((rows * slots,), jnp.int32),
-            dma, dma,
+            dma, dma((rows,)), dma, dma,
         ] + [dma((pieces,))] * 6,
         compiler_params=pltpu.CompilerParams(
             collective_id=0, has_side_effects=True, vmem_limit_bytes=56 * 1024 * 1024),
     )(pattern.reshape(-1), blocks)
+    return 2.0 * halved
 
 
 def solution(mesh):

time: 131 us -> 136 us (1.038)
  other arithmetic: 0 us -> 4.56 us
  local copies, waits for them, and re-layouts: 5.62 us -> 1.13 us
  Pallas kernels: 125 us -> 129 us
    mul x0 -> x1, other arithmetic: none -> 4.56 us  [body(): return 2.0 * halved]
    unnamed x3 -> x2, local copies, waits for them, and re-layouts: 4.78 us -> 0.29 us
    pallas_call x1, Pallas kernels: 125 us -> 129 us  [body(): pl.pallas_call(functools.partial(purify_kernel, lax.axis_size('row'), tot...]
where the time goes in v3:
time: 136 us; the launch traced here: 135 us
  Pallas kernels  129 us (95%)
  other arithmetic  4.56 us (3%)
    pallas_call x1, Pallas kernels, body(): pl.pallas_call(functools.partial(purify_kernel, lax.axis_size('row'), tot...  129 us
    mul x1, other arithmetic, body(): return 2.0 * halved  4.56 us

profile of v3, /device:TPU:0, one launch (start us, length us, event | category | flops | bytes accessed | tf_op | source)
XLA Modules:
  0.0 135.5 jit_solution(3655956431345462308)
XLA Ops:
  0.0 0.0 copy-start
  0.7 0.3 copy-done
  1.0 0.1 copy.4
  1.1 0.7 reshape.7.pattern
  1.8 129.1 %shard_map.37 = f32[6,10,128,128]{3,2,1,0:T(8,128)} custom-call(s32[960]{0:T(1024)} %reshape.7.pattern, f32[60,128,128]{2,1,0:T(8,128)} %bitcast.5), custom_call_target="tpu_custom_call" | custom-call | tf_op jit(solution)/shard_map/pallas_call | solution.py:263
  130.9 4.6 %broadcast_multiply_fusion = f32[6,10,128,128]{3,2,1,0:T(8,128)} fusion(f32[6,10,128,128]{3,2,1,0:T(8,128)} %shard_map.37), kind=kLoop, calls=%fused_computation | loop fusion | flops 983040 | bytes 7864320 | tf_op jit(solution)/shard_map/mul | solution.py:283
  (1 shorter events, 0.0 us)
Async XLA Ops:
  0.0 1.0 copy-start
